TPU v7x, 128 devices: a whole 4x4x4 slice. The times are simulated.
128 devices in a mesh: grp: 2 (over core), ep: 64 (over z, y, x).
Axes of the slice: x: 4, y: 4, z: 4, core: 2. Of those that a mesh axis runs over, the one named last changes fastest.
Arguments:
- hidden_states: bfloat16 [2, 512, 7168], P(None, ('grp', 'ep')), may hold values from -6 to 6
- expert_routes: int32 [2, 512, 8], P(None, ('grp', 'ep')), may hold values from 0 to 15, all different within a row; in each aligned block of 4 rows (0 to 3, 4 to 7, ..., all dimensions but the last counted through in order) at most 4 rows name the same one
- route_gates: bfloat16 [2, 512, 8], P(None, ('grp', 'ep')), may hold values from 0.099609375 to 0.59765625
- gate_weights: bfloat16 [64, 7168, 512], P('ep', None, 'grp'), may hold values from -0.0625 to 0.0625
- up_weights: bfloat16 [64, 7168, 512], P('ep', None, 'grp'), may hold values from -0.0625 to 0.0625
- down_weights: bfloat16 [64, 512, 7168], P('ep', 'grp'), may hold values from -0.125 to 0.125
Outputs:
- mixed: bfloat16 [2, 512, 7168], P(None, ('grp', 'ep'))
Inputs may be any that keep to these rules, and one draw needn't show every extreme that they name: `expert_routes`: each token names 8 different experts. Among the tokens of one block of 4 tokens of a step, no expert is named more than 4 times, and in every draw some expert is named exactly 4 times in some block.
All inputs are finite; a program needn't handle non-finite values.
Results may differ from a plain program's by a relative error of at most 0.015.
Values may be sent and summed in bfloat16 or wider, within the bound.
A program may use at most 128 MiB of HBM per device.

v0:
```python
import jax
import jax.numpy as jnp
from jax import lax
from jax.sharding import PartitionSpec as P

HID = 2048
HID_DEV = 256


def tables(routes, gates, experts, capacity):
    tok_count, topk = routes.shape
    flat_routes = routes.reshape(-1)
    one_hot = (flat_routes[:, None] == jnp.arange(experts, dtype=jnp.int32)[None, :]).astype(
        jnp.int32
    )
    before = jnp.cumsum(one_hot, axis=0) - one_hot
    slot_place = jnp.sum(before * one_hot, axis=1)
    column = flat_routes * capacity + slot_place
    picked = column[:, None] == jnp.arange(experts * capacity, dtype=jnp.int32)[None, :]
    picked = picked.reshape(tok_count, topk, experts * capacity)
    dispatch_table = jnp.any(picked, axis=1)
    combine_table = jnp.sum(
        picked.astype(jnp.float32) * gates.astype(jnp.float32)[:, :, None], axis=1
    )
    return (dispatch_table, combine_table)


def expert_hidden(rows, gate_weights, up_weights):
    flat_rows = rows.reshape(-1, rows.shape[-1])
    gate_proj = jnp.dot(flat_rows, gate_weights[0], preferred_element_type=jnp.float32)
    up_proj = jnp.dot(flat_rows, up_weights[0], preferred_element_type=jnp.float32)
    act = (jax.nn.silu(gate_proj) * up_proj).astype(jnp.bfloat16)
    return act.reshape(rows.shape[:-1] + (gate_weights.shape[2],))


def decode_rows(token_rows, route_rows, gate_rows, gate_weights, up_weights, down_weights):
    n_ep = lax.axis_size("ep")
    n_grp = lax.axis_size("grp")
    holders = HID // (HID_DEV * n_grp)
    experts = n_ep // holders
    step_count, tok_count, width = token_rows.shape
    topk = route_rows.shape[2]
    capacity = max(2, 2 * tok_count * topk // experts)
    local_tables = jax.vmap(lambda r, g: tables(r, g, experts, capacity))
    dispatch_table, combine_table = local_tables(route_rows, gate_rows)
    outgoing = jnp.einsum(
        "stm,std->msd",
        dispatch_table.astype(jnp.bfloat16),
        token_rows,
        preferred_element_type=jnp.float32,
    ).astype(jnp.bfloat16)
    outgoing = outgoing.reshape(experts, 1, capacity, step_count, width)
    outgoing = jnp.broadcast_to(outgoing, (experts, holders, capacity, step_count, width)).reshape(
        n_ep, capacity, step_count, width
    )
    arrived = lax.all_to_all(outgoing, "ep", split_axis=0, concat_axis=0, tiled=True)
    inner_rows = expert_hidden(
        lax.all_gather(arrived, "grp", axis=0, tiled=True), gate_weights, up_weights
    )
    summed = lax.psum_scatter(
        jnp.einsum(
            "acsh,hd->acsd", inner_rows, down_weights[0], preferred_element_type=jnp.float32
        ).astype(jnp.bfloat16),
        "grp",
        scatter_dimension=0,
        tiled=True,
    )
    returned = lax.all_to_all(summed, "ep", split_axis=0, concat_axis=0, tiled=True)
    split_parts = returned.reshape(experts, holders, capacity, step_count, width).astype(
        jnp.float32
    )
    expert_out = jnp.sum(split_parts, axis=1).astype(jnp.bfloat16)
    expert_flat = expert_out.reshape(experts * capacity, step_count, width).astype(jnp.float32)
    mixed = jnp.einsum("stm,msd->std", combine_table, expert_flat, precision=lax.Precision.HIGHEST)
    return mixed.astype(jnp.bfloat16)


def body(hidden_states, expert_routes, route_gates, gate_weights, up_weights, down_weights):
    step_outputs = []
    for step_index in range(hidden_states.shape[0]):
        step_outputs.append(
            decode_rows(
                hidden_states[step_index : step_index + 1],
                expert_routes[step_index : step_index + 1],
                route_gates[step_index : step_index + 1],
                gate_weights,
                up_weights,
                down_weights,
            )
        )
    return jnp.concatenate(step_outputs, axis=0)


def solution(mesh):
    return jax.shard_map(
        body,
        mesh=mesh,
        in_specs=(
            P(None, ("grp", "ep"), None),
            P(None, ("grp", "ep"), None),
            P(None, ("grp", "ep"), None),
            P("ep", None, "grp"),
            P("ep", None, "grp"),
            P("ep", "grp", None),
        ),
        out_specs=P(None, ("grp", "ep"), None),
        check_vma=False,
    )
```

profile of v0, /device:TPU:1, one launch (start us, length us, event | category | flops | bytes accessed | tf_op | source)
XLA Modules:
  0.0 316.7 jit_solution(6334294785129759473)
XLA Ops:
  6.5 0.7 fusion.38
  8.2 0.7 bitcast_add_fusion.1
  9.0 1.3 fusion.3
  10.3 0.3 broadcast_in_dim.29
  10.6 1.1 broadcast_in_dim.30
  11.8 57.3 %all_to_all.20 = bf16[64,4,1,7168]{3,1,2,0:T(4,128)(2,1)} all-to-all(bf16[64,4,1,7168]{3,1,2,0:T(4,128)(2,1)S(1)} %bitcast.82), channel_id=1, replica_groups=mesh['grp'=2,'ep'=64] {'ep'}, dimensions={0} | all-to-all | bytes 7340032 | tf_op jit(solution)/shard_map/all_to_all | solution.py:56
  69.2 0.8 copy-done.2
  70.0 0.5 fusion.2
  70.8 1.1 broadcast_in_dim.13
  71.9 52.4 %all_to_all.21 = bf16[64,4,1,7168]{3,1,2,0:T(4,128)(2,1)} all-to-all(bf16[64,4,1,7168]{3,1,2,0:T(4,128)(2,1)S(1)} %bitcast.83), channel_id=1, replica_groups=mesh['grp'=2,'ep'=64] {'ep'}, dimensions={0} | all-to-all | bytes 7340032 | tf_op jit(solution)/shard_map/all_to_all | solution.py:56
  124.6 12.3 %reshape.410 = bf16[512,7168]{1,0:T(8,128)(2,1)} reshape(bf16[128,4,1,7168]{3,1,2,0:T(4,128)(2,1)} %all-gather.5.cloned.1.call-done) | data formatting | bytes 14680064 | tf_op jit(solution)/shard_map/reshape | solution.py:29
  137.0 7.5 %fusion.12 = f32[512,256]{1,0:T(8,128)S(1)} fusion(bf16[512,7168]{1,0:T(8,128)(2,1)} %reshape.410, bf16[1,7168,256]{2,1,0:T(8,128)(2,1)} %param.9), kind=kOutput, calls=%fused_computation.18 | convolution fusion | flops 1879048192 | bytes 11534336 | tf_op jit(solution)/shard_map/dot_general | solution.py:30
  144.5 0.9 copy-done.4
  145.4 2.1 fusion.22
  147.6 7.2 %fusion.1 = bf16[128,4,1,7168]{3,0,1,2:T(8,128)(2,1)} fusion(bf16[1,256,7168]{2,1,0:T(8,128)(2,1)} %param.11, bf16[128,4,256]{2,1,0:T(4,128)(2,1)S(1)} %reshape.411), kind=kOutput, calls=%fused_computation.3 | convolution fusion | flops 1882718208 | bytes 11272192 | tf_op jit(solution)/shard_map/acsh,hd->acsd/dot_general | solution.py:61
  155.1 12.3 %reshape.405 = bf16[512,7168]{1,0:T(8,128)(2,1)} reshape(bf16[128,4,1,7168]{3,1,2,0:T(4,128)(2,1)} %all-gather.3.cloned.1.call-done) | data formatting | bytes 14680064 | tf_op jit(solution)/shard_map/reshape | solution.py:29
  167.4 7.3 %fusion.14 = f32[512,256]{1,0:T(8,128)S(1)} fusion(bf16[512,7168]{1,0:T(8,128)(2,1)} %reshape.405, bf16[1,7168,256]{2,1,0:T(8,128)(2,1)} %param.9), kind=kOutput, calls=%fused_computation.20 | convolution fusion | flops 1879048192 | bytes 11534336 | tf_op jit(solution)/shard_map/dot_general | solution.py:30
  174.8 1.0 copy-done.5
  175.9 2.1 fusion.25
  178.0 7.1 %fusion = bf16[128,4,1,7168]{3,0,1,2:T(8,128)(2,1)} fusion(bf16[1,256,7168]{2,1,0:T(8,128)(2,1)} %param.11, bf16[128,4,256]{2,1,0:T(4,128)(2,1)S(1)} %reshape.406), kind=kOutput, calls=%fused_computation.2 | convolution fusion | flops 1882718208 | bytes 11272192 | tf_op jit(solution)/shard_map/acsh,hd->acsd/dot_general | solution.py:61
  185.2 6.8 %copy.28 = bf16[64,4,1,7168]{3,1,2,0:T(4,128)(2,1)} copy(bf16[64,4,1,7168]{3,0,1,2:T(8,128)(2,1)} %reduce-scatter.5.cloned.1.call-done) | data formatting | bytes 7340032 | tf_op jit(solution)/shard_map/reduce_scatter | solution.py:60
  191.9 9.3 %all-to-all-start.3 = ((bf16[64,4,1,7168]{3,1,2,0:T(4,128)(2,1)}), bf16[64,4,1,7168]{3,1,2,0:T(4,128)(2,1)}, u32[]{:S(2)}, u32[]{:S(2)}) async-start(bf16[64,4,1,7168]{3,1,2,0:T(4,128)(2,1)} %copy.28), calls=%async_computation.5 | async-start | bytes 7340032 | tf_op jit(solution)/shard_map/all_to_all | solution.py:68
  201.3 2.7 reduce-scatter.3.cloned.1.call-done
  204.0 6.7 %copy.24 = bf16[64,4,1,7168]{3,1,2,0:T(4,128)(2,1)} copy(bf16[64,4,1,7168]{3,0,1,2:T(8,128)(2,1)} %reduce-scatter.3.cloned.1.call-done) | data formatting | bytes 7340032 | tf_op jit(solution)/shard_map/reduce_scatter | solution.py:60
  210.7 37.5 %all-to-all-done.3 = bf16[64,4,1,7168]{3,1,2,0:T(4,128)(2,1)} async-done(((bf16[64,4,1,7168]{3,1,2,0:T(4,128)(2,1)}), bf16[64,4,1,7168]{3,1,2,0:T(4,128)(2,1)}, u32[]{:S(2)}, u32[]{:S(2)}) %all-to-all-start.3) | async-done | bytes 3670048 | tf_op jit(solution)/shard_map/all_to_all | solution.py:68
  248.2 8.9 %all-to-all-start.1 = ((bf16[64,4,1,7168]{3,1,2,0:T(4,128)(2,1)}), bf16[64,4,1,7168]{3,1,2,0:T(4,128)(2,1)}, u32[]{:S(2)}, u32[]{:S(2)}) async-start(bf16[64,4,1,7168]{3,1,2,0:T(4,128)(2,1)} %copy.24), calls=%async_computation.2 | async-start | bytes 7340032 | tf_op jit(solution)/shard_map/all_to_all | solution.py:68
  257.3 4.3 %reduce_sum.71 = bf16[16,4,7168]{2,1,0:T(4,128)(2,1)S(1)} reduce(bf16[16,4,4,7168]{3,2,1,0:T(4,128)(2,1)} %bitcast.22, bf16[]{:T(256)} %constant.22.clone.1), dimensions={1}, to_apply=%region_11.12 | reduce | flops 1376256 | bytes 4587522 | tf_op jit(solution)/shard_map/reduce_sum | solution.py:72
  261.8 42.2 %all-to-all-done.1 = bf16[64,4,1,7168]{3,1,2,0:T(4,128)(2,1)} async-done(((bf16[64,4,1,7168]{3,1,2,0:T(4,128)(2,1)}), bf16[64,4,1,7168]{3,1,2,0:T(4,128)(2,1)}, u32[]{:S(2)}, u32[]{:S(2)}) %all-to-all-start.1) | async-done | bytes 3670048 | tf_op jit(solution)/shard_map/all_to_all | solution.py:68
  304.0 4.3 %reduce_sum.67 = bf16[16,4,7168]{2,1,0:T(4,128)(2,1)S(1)} reduce(bf16[16,4,4,7168]{3,2,1,0:T(4,128)(2,1)} %bitcast.12, bf16[]{:T(256)} %constant.22.clone.1), dimensions={1}, to_apply=%region_5.6 | reduce | flops 1376256 | bytes 4587522 | tf_op jit(solution)/shard_map/reduce_sum | solution.py:72
  308.5 0.5 fusion.5
  309.0 0.5 fusion.4
  309.5 0.7 pad_maximum_fusion
  (38 shorter events, 2.8 us)
Async XLA Ops:
  6.5 118.1 %all-gather.5.cloned.1.call-start = ((), (), s32[]{:S(2)}) async-start(), calls=%async_computation.8 | async-start | bytes 11010048 | tf_op jit(solution)/shard_map/all_gather | solution.py:58
  69.1 0.9 copy-start.2
  69.1 85.9 %all-gather.3.cloned.1.call-start = ((), (), s32[]{:S(2)}) async-start(), calls=%async_computation.6 | async-start | bytes 11010048 | tf_op jit(solution)/shard_map/all_gather | solution.py:58
  124.4 60.8 %reduce-scatter.5.cloned.1.call-start = ((), (), s32[]{:S(2)}) async-start(), calls=%async_computation.9 | async-start | bytes 11010048 | tf_op jit(solution)/shard_map/reduce_scatter | solution.py:60
  137.0 7.5 %copy-start = (bf16[512,7168]{1,0:T(8,128)(2,1)S(1)}, bf16[512,7168]{1,0:T(8,128)(2,1)}, u32[]{:S(2)}) copy-start(bf16[512,7168]{1,0:T(8,128)(2,1)} %reshape.410) | copy-start | bytes 22020100
  137.0 8.5 %copy-start.4 = (bf16[1,7168,256]{2,1,0:T(8,128)(2,1)S(1)}, bf16[1,7168,256]{2,1,0:T(8,128)(2,1)}, u32[]{:S(2)}) copy-start(bf16[1,7168,256]{2,1,0:T(8,128)(2,1)} %param.10) | copy-start | bytes 11010052
  154.8 49.3 %reduce-scatter.3.cloned.1.call-start = ((), (), s32[]{:S(2)}) async-start(), calls=%async_computation.7 | async-start | bytes 11010048 | tf_op jit(solution)/shard_map/reduce_scatter | solution.py:60
  167.4 7.5 %copy-start.1 = (bf16[512,7168]{1,0:T(8,128)(2,1)S(1)}, bf16[512,7168]{1,0:T(8,128)(2,1)}, u32[]{:S(2)}) copy-start(bf16[512,7168]{1,0:T(8,128)(2,1)} %reshape.405) | copy-start | bytes 22020100
  167.4 8.5 %copy-start.5 = (bf16[1,7168,256]{2,1,0:T(8,128)(2,1)S(1)}, bf16[1,7168,256]{2,1,0:T(8,128)(2,1)}, u32[]{:S(2)}) copy-start(bf16[1,7168,256]{2,1,0:T(8,128)(2,1)} %param.10) | copy-start | bytes 11010052
  191.9 56.3 %all-to-all-start.3 = ((bf16[64,4,1,7168]{3,1,2,0:T(4,128)(2,1)}), bf16[64,4,1,7168]{3,1,2,0:T(4,128)(2,1)}, u32[]{:S(2)}, u32[]{:S(2)}) async-start(bf16[64,4,1,7168]{3,1,2,0:T(4,128)(2,1)} %copy.28), calls=%async_computation.5 | async-start | bytes 7340032 | tf_op jit(solution)/shard_map/all_to_all | solution.py:68
  210.7 46.5 %copy-start.3 = (bf16[2,4,8]{2,1,0:T(4,128)(2,1)S(1)}, bf16[2,4,8]{2,1,0:T(4,128)(2,1)}, u32[]{:S(2)}) copy-start(bf16[2,4,8]{2,1,0:T(4,128)(2,1)} %param.8) | copy-start | bytes 388
  248.2 55.8 %all-to-all-start.1 = ((bf16[64,4,1,7168]{3,1,2,0:T(4,128)(2,1)}), bf16[64,4,1,7168]{3,1,2,0:T(4,128)(2,1)}, u32[]{:S(2)}, u32[]{:S(2)}) async-start(bf16[64,4,1,7168]{3,1,2,0:T(4,128)(2,1)} %copy.24), calls=%async_computation.2 | async-start | bytes 7340032 | tf_op jit(solution)/shard_map/all_to_all | solution.py:68
Sparse Core Ops, SparseCore 0:
  69.3 19.3 all-gather.4
  124.5 19.1 all-gather.2
  154.9 17.7 reduce-scatter.4
  185.3 18.7 reduce-scatter.2
where the time goes:
time: 319 us; the launch traced here: 317 us
  blocking collectives  110 us (34%)
  waiting for transfers between devices  82.6 us (26%)
  local copies, waits for them, and re-layouts  45.5 us (14%)
  matrix products  35.9 us (11%)
  starting transfers between devices  18.8 us (6%)
  between operations  13.3 us (4%)
  other arithmetic  10.9 us (3%)
    all_to_all x2, blocking collectives, decode_rows(): lax.all_to_all(outgoing, 'ep', split_axis=0, concat_axis=0, tiled=True)  110 us
    all_to_all x2, waiting for transfers between devices, decode_rows(): lax.all_to_all(summed, 'ep', split_axis=0, concat_axis=0, tiled=True)  79.7 us
    reshape x2, local copies, waits for them, and re-layouts, expert_hidden(): flat_rows = rows.reshape(-1, rows.shape[-1])  24.7 us
    all_to_all x2, starting transfers between devices, decode_rows(): lax.all_to_all(summed, 'ep', split_axis=0, concat_axis=0, tiled=True)  18.3 us
    dot_general x2, matrix products, expert_hidden(): jnp.dot(flat_rows, gate_weights[0], preferred_element_type=jnp.float32)  14.8 us
    dot_general x2, matrix products, decode_rows(): jnp.einsum('acsh,hd->acsd', inner_rows, down_weights[0], preferred_elemen...  14.2 us
    reduce_scatter x2, local copies, waits for them, and re-layouts, decode_rows(): lax.psum_scatter(jnp.einsum('acsh,hd->acsd', inner_rows, down_weights[0],...  13.5 us
    reduce_sum x2, other arithmetic, decode_rows(): expert_out = jnp.sum(split_parts, axis=1).astype(jnp.bfloat16)  8.6 us
  transfers between devices with their start and end apart: 6, of which 3 were waited for; matrix products, arithmetic and copies ran while one was open for 25% of the time, Pallas kernels for 0%

commit v1 on v0

v1 whole, which is shorter than its diff:
```python
import jax
import jax.numpy as jnp
from jax import lax
from jax.sharding import PartitionSpec as P

EXPERTS = 16
PAD = 128


def expert_weights(routes, gates):
    picked = routes[..., None] == jnp.arange(EXPERTS, dtype=jnp.int32)
    return jnp.sum(
        jnp.where(picked, gates.astype(jnp.float32)[..., None], 0.0), axis=-2
    ).astype(jnp.bfloat16)


def body(hidden_states, expert_routes, route_gates, gate_weights, up_weights, down_weights):
    steps, tok, width = hidden_states.shape
    holders = lax.axis_size("ep") // EXPERTS
    mine = lax.axis_index("ep") // holders
    table = expert_weights(expert_routes, route_gates)
    table = jnp.pad(table, ((0, 0), (0, 0), (0, PAD - EXPERTS)))
    rows = jnp.concatenate([hidden_states, table], axis=-1)
    outs = []
    for s in range(steps):
        full = lax.all_gather(rows[s], ("grp", "ep"), axis=0, tiled=True)
        x = full[:, :width]
        weight = jnp.sum(
            jnp.where(
                jnp.arange(PAD) == mine, full[:, width:].astype(jnp.float32), 0.0
            ),
            axis=1,
            keepdims=True,
        )
        gate = jnp.dot(x, gate_weights[0], preferred_element_type=jnp.float32)
        up = jnp.dot(x, up_weights[0], preferred_element_type=jnp.float32)
        act = (jax.nn.silu(gate) * up).astype(jnp.bfloat16)
        part = jnp.dot(act, down_weights[0], preferred_element_type=jnp.float32)
        part = (part * weight).astype(jnp.bfloat16)
        outs.append(lax.psum_scatter(part, ("grp", "ep"), scatter_dimension=0, tiled=True))
    return jnp.stack(outs, axis=0)


def solution(mesh):
    return jax.shard_map(
        body,
        mesh=mesh,
        in_specs=(
            P(None, ("grp", "ep"), None),
            P(None, ("grp", "ep"), None),
            P(None, ("grp", "ep"), None),
            P("ep", None, "grp"),
            P("ep", None, "grp"),
            P("ep", "grp", None),
        ),
        out_specs=P(None, ("grp", "ep"), None),
        check_vma=False,
    )
```

time: 319 us -> 401 us (1.26)
  waiting for transfers between devices: 82.6 us -> 318 us
  blocking collectives: 110 us -> 0 us
  local copies, waits for them, and re-layouts: 45.5 us -> 21.2 us
  starting transfers between devices: 18.8 us -> 0.08 us
  matrix products: 35.9 us -> 44.6 us
  other arithmetic: 10.9 us -> 3.43 us
    unnamed x4, waiting for transfers between devices: 0.07 us -> 173 us
    all_gather x2, waiting for transfers between devices: 0.04 us -> 144 us  [body(): full = lax.all_gather(rows[s], ('grp', 'ep'), axis=0, tiled=True)]
    all_to_all x2 -> x0, blocking collectives: 110 us -> none  [decode_rows(): lax.all_to_all(outgoing, 'ep', split_axis=0, concat_axis=0, tiled=True)]
    all_to_all x2 -> x0, waiting for transfers between devices: 79.7 us -> none  [decode_rows(): lax.all_to_all(summed, 'ep', split_axis=0, concat_axis=0, tiled=True)]
    reshape x2 -> x0, local copies, waits for them, and re-layouts: 24.7 us -> none  [expert_hidden(): flat_rows = rows.reshape(-1, rows.shape[-1])]
    all_to_all x2 -> x0, starting transfers between devices: 18.3 us -> none  [decode_rows(): lax.all_to_all(summed, 'ep', split_axis=0, concat_axis=0, tiled=True)]
    unnamed x12 -> x4, local copies, waits for them, and re-layouts: 2.92 us -> 19.3 us
    reduce_scatter x2 -> x0, local copies, waits for them, and re-layouts: 13.5 us -> none  [decode_rows(): lax.psum_scatter(jnp.einsum('acsh,hd->acsd', inner_rows, down_weights[0],...]
  transfers between devices with their start and end apart: 6 -> 3, of which waited for: 3 -> 3; matrix products, arithmetic and copies ran while one was open for 25% -> 4% of each run, Pallas kernels for 0% -> 0%
where the time goes in v1:
time: 401 us; the launch traced here: 400 us
  waiting for transfers between devices  318 us (79%)
  matrix products  44.6 us (11%)
  local copies, waits for them, and re-layouts  21.2 us (5%)
  between operations  13.2 us (3%)
    unnamed x4, waiting for transfers between devices  173 us
    all_gather x2, waiting for transfers between devices, body(): full = lax.all_gather(rows[s], ('grp', 'ep'), axis=0, tiled=True)  144 us
    dot_general x2, matrix products, body(): part = jnp.dot(act, down_weights[0], preferred_element_type=jnp.float32)  32.1 us
    unnamed x4, local copies, waits for them, and re-layouts  19.3 us
    dot_general x2, matrix products, body(): gate = jnp.dot(x, gate_weights[0], preferred_element_type=jnp.float32)  12.4 us
  transfers between devices with their start and end apart: 3, of which 3 were waited for; matrix products, arithmetic and copies ran while one was open for 4% of the time, Pallas kernels for 0%

profile of v1, /device:TPU:1, one launch (start us, length us, event | category | flops | bytes accessed | tf_op | source)
XLA Modules:
  0.0 400.2 jit_solution(17035913353683333696)
XLA Ops:
  6.5 0.0 all-gather.5.cloned.1.call-start
  6.5 1.0 copy.9
  7.5 0.7 convert_element_type.26
  8.2 0.8 select_reduce_fusion.2
  9.0 0.1 fusion.44
  9.1 0.9 fusion.47
  10.0 0.0 all-gather.5.cloned.1.call-update
  10.0 0.0 all-gather.7.cloned.1.call-start
  10.1 0.7 all-gather.7.cloned.1.call-update
  10.8 0.0 all-reduce.6.cloned.1.call-start
  10.8 80.2 %all-gather.5.cloned.1.call-done = bf16[1,512,7296]{2,0,1:T(2,128)(2,1)} async-done(((bf16[1,4,7296]{2,0,1:T(2,128)(2,1)}), bf16[1,512,7296]{2,0,1:T(2,128)(2,1)}) %all-gather.5.cloned.1.call-update) | async-done | bytes 7471120 | tf_op jit(solution)/shard_map/all_gather | solution.py:26
  91.1 9.2 %copy.17 = bf16[1,512,7296]{2,1,0:T(8,128)(2,1)} copy(bf16[1,512,7296]{2,0,1:T(2,128)(2,1)} %all-gather.5.cloned.1.call-done) | data formatting | bytes 14942208
  100.2 6.3 %fusion.6 = f32[512,256]{1,0:T(8,128)S(1)} fusion(bf16[512,7296]{1,0:T(8,128)(2,1)} %bitcast.37, bf16[1,7168,256]{2,1,0:T(8,128)(2,1)} %param.9), kind=kOutput, calls=%fused_computation.10 | convolution fusion | flops 1879048192 | bytes 11534336 | tf_op jit(solution)/shard_map/dot_general | solution.py:35
  106.5 64.1 %all-gather.7.cloned.1.call-done = bf16[1,512,7296]{2,0,1:T(2,128)(2,1)} async-done(((bf16[1,4,7296]{2,0,1:T(2,128)(2,1)}), bf16[1,512,7296]{2,0,1:T(2,128)(2,1)}) %all-gather.7.cloned.1.call-update) | async-done | bytes 7471120 | tf_op jit(solution)/shard_map/all_gather | solution.py:26
  170.6 9.2 %copy.16 = bf16[1,512,7296]{2,1,0:T(8,128)(2,1)} copy(bf16[1,512,7296]{2,0,1:T(2,128)(2,1)} %all-gather.7.cloned.1.call-done) | data formatting | bytes 14942208
  179.8 6.2 %fusion.2 = f32[512,256]{1,0:T(8,128)S(1)} fusion(bf16[512,7296]{1,0:T(8,128)(2,1)} %bitcast.40, bf16[1,7168,256]{2,1,0:T(8,128)(2,1)} %param.9), kind=kOutput, calls=%fused_computation.6 | convolution fusion | flops 1879048192 | bytes 11534336 | tf_op jit(solution)/shard_map/dot_general | solution.py:35
  186.0 1.1 select_reduce_fusion.1
  187.1 16.0 %multiply_convert_fusion.1 = bf16[512,7168]{1,0:T(8,128)(2,1)} fusion(f32[512]{0:T(512)S(1)} %get-tuple-element.5, bf16[1,256,7168]{2,1,0:T(8,128)(2,1)} %param.11, bf16[1,7168,256]{2,1,0:T(8,128)(2,1)} %param.10, bf16[512,7296]{1,0:T(8,128)(2,1)} %bitcast.39, f32[512,256]{1,0:T(8,128)S(1)} %fusion.6), kind=kOutput, calls=%fused_computation.1 | convolution fusion | flops 3766222848 | bytes 22546432 | tf_op jit(solution)/shard_map/dot_general | solution.py:38
  203.2 16.1 %multiply_convert_fusion = bf16[512,7168]{1,0:T(8,128)(2,1)} fusion(f32[512]{0:T(512)S(1)} %get-tuple-element.6, bf16[1,256,7168]{2,1,0:T(8,128)(2,1)} %param.11, bf16[1,7168,256]{2,1,0:T(8,128)(2,1)} %param.10, bf16[512,7296]{1,0:T(8,128)(2,1)} %bitcast.42, f32[512,256]{1,0:T(8,128)S(1)} %fusion.2), kind=kOutput, calls=%fused_computation | convolution fusion | flops 3766222848 | bytes 22546432 | tf_op jit(solution)/shard_map/dot_general | solution.py:38
  219.2 0.0 all-reduce.6.cloned.1.call-update
  219.3 172.7 %all-reduce.6.cloned.1.call-done = (bf16[512,7168]{1,0:T(8,128)(2,1)}, bf16[512,7168]{1,0:T(8,128)(2,1)}) async-done(((bf16[512,7168]{1,0:T(8,128)(2,1)}, bf16[512,7168]{1,0:T(8,128)(2,1)}), (bf16[512,7168]{1,0:T(8,128)(2,1)}, bf16[512,7168]{1,0:T(8,128)(2,1)})) %all-reduce.6.cloned.1.call-update) | async-done | bytes 14680080
  392.0 1.0 dynamic-slice_bitcast_fusion
  393.0 0.7 pad_maximum_fusion
  (2 shorter events, 0.0 us)
Async XLA Ops:
  6.5 84.5 %all-gather.5.cloned.1.call-start = ((), (), s32[]{:S(2)}) async-start(), calls=%async_computation | async-start | bytes 15058944 | tf_op jit(solution)/shard_map/all_gather | solution.py:26
  10.0 160.6 %all-gather.7.cloned.1.call-start = ((), (), s32[]{:S(2)}) async-start(), calls=%async_computation.1 | async-start | bytes 15058944 | tf_op jit(solution)/shard_map/all_gather | solution.py:26
  10.8 381.2 %all-reduce.6.cloned.1.call-start = ((), (), s32[]{:S(2)}) async-start(), calls=%async_computation.2 | async-start | bytes 29360128
Sparse Core Ops, SparseCore 0:
  10.3 80.7 all-gather.4
  94.0 76.5 all-gather.6
  219.4 172.5 all-reduce.5

commit v2 on v1

v2 whole, which is shorter than its diff:
```python
import jax
import jax.numpy as jnp
from jax import lax
from jax.experimental import pallas as pl
from jax.experimental.pallas import tpu as pltpu
from jax.sharding import PartitionSpec as P

EXPERTS = 16
LANE = 128
TILE = 16
UNITS = 28
HALF = UNITS * LANE
HALF_T = HALF + LANE
HIDDEN = 256
MESH = pl.DeviceIdType.MESH
F32 = jnp.float32
BF16 = jnp.bfloat16

PARTS = ((0, 10, (2, 1, 0)), (10, 9, (0, 2, 1)), (19, 9, (1, 0, 2)))
TABLE_PART = 2


def part_units(p, table):
    first, count, _ = PARTS[p]
    return first, count + (1 if table and p == TABLE_PART else 0)


def halves(p, table):
    first, count = part_units(p, table)
    left = (count + 1) // 2
    return (first, left), (first + left, count - left)


def kernel(
    hs, routes, gates, wg_hbm, wu_hbm, wd_hbm,
    out,
    X, wgu, wd, h, act, zero_send, zero_recv, last_send, last_recv, R0,
    R30, R31, R32, R20, R21, R22, R10, R11, R12,
    w_sem, g_send, g_recv, b_send, b_recv, s_send, s_recv, c_send, c_recv, e_send, e_recv,
):
    R = {3: (R30, R31, R32), 2: (R20, R21, R22), 1: (R10, R11, R12)}
    core = lax.axis_index("grp")
    ep = lax.axis_index("ep")
    me = (ep // 16, (ep // 4) % 4, ep % 4)
    sibling = (1 - core, ep)
    scale = (16, 4, 1)

    def peer(axis, delta):
        moved = lax.rem(me[axis] + delta, 4)
        return (core, ep + (moved - me[axis]) * scale[axis])

    def place(axis, delta):
        return lax.rem(me[axis] + delta, 4)

    weights = [
        pltpu.make_async_copy(wg_hbm.at[0], wgu.at[:, pl.ds(0, HIDDEN)], w_sem.at[0]),
        pltpu.make_async_copy(wu_hbm.at[0], wgu.at[:, pl.ds(HIDDEN, HIDDEN)], w_sem.at[1]),
        pltpu.make_async_copy(wd_hbm.at[0], wd, w_sem.at[2]),
    ]
    for copy in weights:
        copy.start()

    barrier = pltpu.get_barrier_semaphore()
    for axis in range(3):
        for delta in (1, 3):
            pl.semaphore_signal(barrier, inc=1, device_id=peer(axis, delta), device_id_type=MESH)
    pl.semaphore_signal(barrier, inc=1, device_id=sibling, device_id_type=MESH)

    lane = lax.broadcasted_iota(jnp.int32, (4, LANE), 1)

    def own_rows(c):
        at = pl.multiple_of(c * HALF, LANE)
        return jnp.concatenate(
            [hs[s, :, pl.ds(at, HALF)].astype(F32) for s in range(2)], axis=0
        )

    tables = []
    for s in range(2):
        total = jnp.zeros((4, LANE), F32)
        for k in range(8):
            total += jnp.where(
                lane == routes[s, :, k : k + 1], gates[s, :, k : k + 1].astype(F32), 0.0
            )
        tables.append(total)
    table = jnp.concatenate(tables, axis=0)

    zero_send[:, pl.ds(0, HALF)] = own_rows(1 - core)
    zero_send[:, pl.ds(HALF, LANE)] = table
    pl.semaphore_wait(barrier, 7)
    swap = pltpu.make_async_remote_copy(
        src_ref=zero_send, dst_ref=zero_recv, send_sem=e_send.at[0], recv_sem=e_recv.at[0],
        device_id=sibling, device_id_type=MESH,
    )
    swap.start()
    h[...] = jnp.zeros_like(h)
    base = pl.multiple_of(core * HALF_T, LANE)
    mine = jnp.concatenate([own_rows(core), table], axis=1)
    swap.wait()
    theirs = zero_recv[...]
    first = core == 0
    X[me[0], me[1], me[2], :, pl.ds(base, HALF_T)] = jnp.concatenate(
        [jnp.where(first, mine, theirs), jnp.where(first, theirs, mine)], axis=0
    ).astype(BF16)

    def block(p, stage, j, c, first_unit, count):
        order = PARTS[p][2]
        index = []
        for axis in range(3):
            if axis == order[stage - 1]:
                index.append(pl.ds(j, 1))
            elif axis in order[: stage - 1]:
                index.append(pl.ds(0, 4))
            else:
                index.append(pl.ds(me[axis], 1))
        at = pl.multiple_of(c * HALF_T + first_unit * LANE, LANE)
        return tuple(index) + (pl.ds(0, TILE), pl.ds(at, count * LANE))

    def gather_copy(p, stage, k, j, half, device):
        ref = X.at[block(p, stage, j, core, *half)]
        at = ((stage - 1) * 3 + p) * 6 + k
        return pltpu.make_async_remote_copy(
            src_ref=ref, dst_ref=ref, send_sem=g_send.at[at], recv_sem=g_recv.at[at],
            device_id=device, device_id_type=MESH,
        )

    def gather_message(p, stage, k, arriving):
        axis = PARTS[p][2][stage - 1]
        a, b = halves(p, True)
        offset, half, to = (
            (0, a, 1), (0, b, 1), (0, b, 3), (0, a, 3), (3, a, 1), (1, b, 3)
        )[k]
        if arriving:
            offset = offset + (3 if to == 1 else 1)
        return gather_copy(p, stage, k, place(axis, offset), half, peer(axis, to))

    def gather_start(p, stage):
        for k in (0, 2, 1, 3):
            gather_message(p, stage, k, False).start()

    def gather_arrived(p, stage, k):
        gather_message(p, stage, k, True).wait_recv()

    def gather_forward(p, stage):
        gather_arrived(p, stage, 0)
        gather_message(p, stage, 4, False).start()
        gather_arrived(p, stage, 2)
        gather_message(p, stage, 5, False).start()

    for stage in (1, 2):
        for p in range(3):
            gather_start(p, stage)
        for p in range(3):
            gather_forward(p, stage)
        for p in range(3):
            for k in (1, 3, 4, 5):
                gather_arrived(p, stage, k)

    def pass_copy(p, k, c):
        axis = PARTS[p][2][2]
        offset = (0, 3, 1, 2, 2)[k]
        part = (PARTS[p][0], PARTS[p][1])
        cut = (part, part, part) + halves(p, False)
        ref = X.at[block(p, 3, place(axis, offset), c, *cut[k])]
        at = p * 5 + k
        return pltpu.make_async_remote_copy(
            src_ref=ref, dst_ref=ref, send_sem=s_send.at[at], recv_sem=s_recv.at[at],
            device_id=sibling, device_id_type=MESH,
        )

    def hidden_index(p, j):
        axis = PARTS[p][2][2]
        return tuple(pl.ds(j, 1) if a == axis else pl.ds(0, 4) for a in range(3))

    def multiply(p, offset, c):
        first_unit, count, order = PARTS[p]
        j = place(order[2], offset)
        rows = X[block(p, 3, j, c, first_unit, count)].reshape(16 * TILE, count * LANE)
        at = pl.multiple_of(c * HALF + first_unit * LANE, LANE)
        where = hidden_index(p, j)
        found = jnp.dot(rows, wgu[pl.ds(at, count * LANE), :], preferred_element_type=F32)
        h[where] += found.reshape(h[where].shape)

    for p in range(3):
        gather_start(p, 3)
    for p in range(3):
        pass_copy(p, 0, core).start()
    weights[0].wait()
    weights[1].wait()
    for p in range(3):
        multiply(p, 0, core)
    for p in range(3):
        pass_copy(p, 0, 1 - core).wait_recv()
        multiply(p, 0, 1 - core)
    for p in range(3):
        gather_forward(p, 3)
    for p in range(3):
        gather_arrived(p, 3, 1)
        pass_copy(p, 1, core).start()
        gather_arrived(p, 3, 3)
        pass_copy(p, 2, core).start()
    for p in range(3):
        multiply(p, 3, core)
        multiply(p, 1, core)
    for p in range(3):
        pass_copy(p, 1, 1 - core).wait_recv()
        multiply(p, 3, 1 - core)
        pass_copy(p, 2, 1 - core).wait_recv()
        multiply(p, 1, 1 - core)
    for p in range(3):
        gather_arrived(p, 3, 4)
        pass_copy(p, 3, core).start()
        gather_arrived(p, 3, 5)
        pass_copy(p, 4, core).start()
    for p in range(3):
        multiply(p, 2, core)
    for p in range(3):
        pass_copy(p, 3, 1 - core).wait_recv()
        pass_copy(p, 4, 1 - core).wait_recv()
        multiply(p, 2, 1 - core)

    chosen = (lax.broadcasted_iota(jnp.int32, (LANE, HIDDEN), 0) == ep // 4).astype(BF16)
    table_at = pl.multiple_of(base + HALF, LANE)

    def activate(i, carry):
        rows = X[i, :, :, :, pl.ds(table_at, LANE)].reshape(16 * TILE, LANE)
        scaled = jnp.dot(rows, chosen, preferred_element_type=F32)
        both = h[i].reshape(16 * TILE, 2 * HIDDEN)
        gate, up = both[:, :HIDDEN], both[:, HIDDEN:]
        value = gate / (1.0 + jnp.exp(-gate)) * up * scaled
        act[i] = value.astype(BF16).reshape(4, 4, TILE, HIDDEN)
        return carry

    lax.fori_loop(0, 4, activate, 0)

    for stage in (1, 2, 3):
        for p in range(3):
            for k in range(6):
                gather_message(p, stage, k, False).wait_send()
    for p in range(3):
        for k in range(5):
            pass_copy(p, k, core).wait_send()
    weights[2].wait()

    def down(p, offset, c):
        first_unit, count, order = PARTS[p]
        rows = act[hidden_index(p, place(order[2], offset))].reshape(16 * TILE, HIDDEN)
        at = pl.multiple_of(c * HALF + first_unit * LANE, LANE)
        return jnp.dot(rows, wd[:, pl.ds(at, count * LANE)], preferred_element_type=F32)

    def cross_copy(p, offset, c):
        first_unit, count, order = PARTS[p]
        j = place(order[2], offset)
        where = block(p, 3, j, c, first_unit, count)
        to = hidden_index(p, j) + (pl.ds(0, TILE), pl.ds(first_unit * LANE, count * LANE))
        return pltpu.make_async_remote_copy(
            src_ref=X.at[where], dst_ref=R0.at[to],
            send_sem=c_send.at[p * 4 + offset], recv_sem=c_recv.at[p * 4 + offset],
            device_id=sibling, device_id_type=MESH,
        )

    def theirs_out(p, offset):
        first_unit, count, order = PARTS[p]
        where = block(p, 3, place(order[2], offset), 1 - core, first_unit, count)
        X[where] = down(p, offset, 1 - core).astype(BF16).reshape(X[where].shape)
        cross_copy(p, offset, 1 - core).start()

    def mine_out(p, offset):
        first_unit, count, order = PARTS[p]
        j = place(order[2], offset)
        where = block(p, 3, j, core, first_unit, count)
        found = down(p, offset, core)
        cross_copy(p, offset, core).wait_recv()
        to = hidden_index(p, j) + (pl.ds(0, TILE), pl.ds(first_unit * LANE, count * LANE))
        X[where] = (found.reshape(X[where].shape) + R0[to].astype(F32)).astype(BF16)

    def scatter_message(p, stage, k, arriving=False):
        order = PARTS[p][2]
        axis = order[stage - 1]
        a, b = halves(p, False)
        offset, half, to, slot = (
            (2, a, 1, 0), (2, b, 3, 0), (1, b, 1, 1), (3, a, 3, 2), (1, a, 1, 1), (3, b, 3, 2)
        )[k]
        src = X.at[block(p, stage, place(axis, offset), core, *half)]
        buffer = R[stage][p]
        span = (pl.ds((half[0] - PARTS[p][0]) * LANE, half[1] * LANE),)
        dst = buffer.at[(slot, slice(None), slice(None), slice(None), slice(None)) + span]
        at = ((stage - 1) * 3 + p) * 6 + k
        return pltpu.make_async_remote_copy(
            src_ref=src, dst_ref=dst, send_sem=b_send.at[at], recv_sem=b_recv.at[at],
            device_id=peer(axis, to), device_id_type=MESH,
        )

    def accumulate(p, stage, offset, half, slots):
        order = PARTS[p][2]
        j = place(order[stage - 1], offset)
        where = block(p, stage, j, core, *half)
        span = pl.ds((half[0] - PARTS[p][0]) * LANE, half[1] * LANE)
        buffer = R[stage][p]
        loops = [a for a in range(3) if a in order[: stage - 1]]

        def add(i, carry):
            at, frm = list(where), [slice(None)] * 3
            if loops:
                at[loops[0]] = pl.ds(i, 1)
                frm[loops[0]] = pl.ds(i, 1)
            at = tuple(at)
            total = X[at].astype(F32)
            for slot in slots:
                total += buffer[(slot,) + tuple(frm) + (slice(None), span)].astype(F32)
            X[at] = total.astype(BF16)
            return carry

        if loops:
            lax.fori_loop(0, 4, add, 0)
        else:
            add(0, 0)

    def scatter_forward(p, stage):
        a, b = halves(p, False)
        scatter_message(p, stage, 0).wait_recv()
        accumulate(p, stage, 1, a, (0,))
        scatter_message(p, stage, 4).start()
        scatter_message(p, stage, 1).wait_recv()
        accumulate(p, stage, 3, b, (0,))
        scatter_message(p, stage, 5).start()

    def scatter_finish(p, stage):
        for k in (2, 3, 4, 5):
            scatter_message(p, stage, k).wait_recv()
        if stage > 1:
            for half in halves(p, False):
                accumulate(p, stage, 0, half, (1, 2))

    for p in range(3):
        theirs_out(p, 2)
    for p in range(3):
        mine_out(p, 2)
        scatter_message(p, 3, 0).start()
        scatter_message(p, 3, 1).start()
    for p in range(3):
        theirs_out(p, 1)
        theirs_out(p, 3)
    for p in range(3):
        mine_out(p, 1)
        scatter_message(p, 3, 2).start()
        mine_out(p, 3)
        scatter_message(p, 3, 3).start()
    for p in range(3):
        scatter_forward(p, 3)
    for p in range(3):
        theirs_out(p, 0)
    for p in range(3):
        mine_out(p, 0)
    for p in range(3):
        scatter_finish(p, 3)
    for stage in (2, 1):
        for p in range(3):
            for k in (0, 1, 2, 3):
                scatter_message(p, stage, k).start()
        for p in range(3):
            scatter_forward(p, stage)
        for p in range(3):
            scatter_finish(p, stage)

    pieces = []
    for p in range(3):
        first_unit, count, order = PARTS[p]
        where = block(p, 1, me[order[0]], core, first_unit, count)
        total = X[where].astype(F32).reshape(TILE, count * LANE)
        for slot in (1, 2):
            total += R[1][p][slot].astype(F32).reshape(TILE, count * LANE)
        pieces.append(total)
    tile = jnp.concatenate(pieces, axis=1)
    last_send[...] = jnp.where(first, tile[8:], tile[:8])
    swap_back = pltpu.make_async_remote_copy(
        src_ref=last_send, dst_ref=last_recv, send_sem=e_send.at[1], recv_sem=e_recv.at[1],
        device_id=sibling, device_id_type=MESH,
    )
    swap_back.start()
    kept = jnp.where(first, tile[:8], tile[8:]).astype(BF16)
    at = pl.multiple_of(core * HALF, LANE)
    for s in range(2):
        out[s, :, pl.ds(at, HALF)] = kept[4 * s : 4 * s + 4]
    for stage in (1, 2, 3):
        for p in range(3):
            for k in range(6):
                scatter_message(p, stage, k).wait_send()
    for p in range(3):
        for offset in range(4):
            cross_copy(p, offset, 1 - core).wait_send()
    swap_back.wait()
    other = last_recv[...].astype(BF16)
    at = pl.multiple_of((1 - core) * HALF, LANE)
    for s in range(2):
        out[s, :, pl.ds(at, HALF)] = other[4 * s : 4 * s + 4]


def scatter_shapes():
    shapes = []
    for stage in (3, 2, 1):
        for p in range(3):
            order = PARTS[p][2]
            dims = tuple(4 if a in order[: stage - 1] else 1 for a in range(3))
            shapes.append(pltpu.VMEM((3,) + dims + (TILE, PARTS[p][1] * LANE), BF16))
    return shapes


def body(hidden_states, expert_routes, route_gates, gate_weights, up_weights, down_weights):
    width = hidden_states.shape[2]
    dma = pltpu.SemaphoreType.DMA
    vmem = pl.BlockSpec(memory_space=pltpu.VMEM)
    hbm = pl.BlockSpec(memory_space=pl.ANY)
    return pl.pallas_call(
        kernel,
        out_shape=jax.ShapeDtypeStruct(hidden_states.shape, BF16),
        in_specs=[vmem, vmem, vmem, hbm, hbm, hbm],
        out_specs=vmem,
        scratch_shapes=[
            pltpu.VMEM((4, 4, 4, TILE, 2 * HALF_T), BF16),
            pltpu.VMEM((width, 2 * HIDDEN), BF16),
            pltpu.VMEM((HIDDEN, width), BF16),
            pltpu.VMEM((4, 4, 4, TILE, 2 * HIDDEN), F32),
            pltpu.VMEM((4, 4, 4, TILE, HIDDEN), BF16),
            pltpu.VMEM((8, HALF_T), F32),
            pltpu.VMEM((8, HALF_T), F32),
            pltpu.VMEM((8, HALF), F32),
            pltpu.VMEM((8, HALF), F32),
            pltpu.VMEM((4, 4, 4, TILE, HALF), BF16),
            *scatter_shapes(),
            dma((3,)),
            dma((54,)), dma((54,)),
            dma((54,)), dma((54,)),
            dma((15,)), dma((15,)),
            dma((12,)), dma((12,)),
            dma((2,)), dma((2,)),
        ],
        compiler_params=pltpu.CompilerParams(
            collective_id=0, has_side_effects=True, vmem_limit_bytes=60 * 1024 * 1024
        ),
        cost_estimate=pl.CostEstimate(
            flops=11_300_000_000, bytes_accessed=12_000_000, transcendentals=262144
        ),
    )(hidden_states, expert_routes, route_gates, gate_weights, up_weights, down_weights)


def solution(mesh):
    return jax.shard_map(
        body,
        mesh=mesh,
        in_specs=(
            P(None, ("grp", "ep"), None),
            P(None, ("grp", "ep"), None),
            P(None, ("grp", "ep"), None),
            P("ep", None, "grp"),
            P("ep", None, "grp"),
            P("ep", "grp", None),
        ),
        out_specs=P(None, ("grp", "ep"), None),
        check_vma=False,
    )
```

time: 401 us -> 102 us (0.25)
  waiting for transfers between devices: 318 us -> 0 us
  Pallas kernels: 0 us -> 100 us
  matrix products: 44.6 us -> 0 us
  local copies, waits for them, and re-layouts: 21.2 us -> 1.59 us
  between operations: 13.2 us -> 0.01 us
    unnamed x4 -> x0, waiting for transfers between devices: 173 us -> none
    all_gather x2 -> x0, waiting for transfers between devices: 144 us -> none  [body(): full = lax.all_gather(rows[s], ('grp', 'ep'), axis=0, tiled=True)]
    pallas_call x0 -> x1, Pallas kernels: none -> 100 us  [body(): pl.pallas_call(kernel, out_shape=jax.ShapeDtypeStruct(hidden_states.shape...]
    dot_general x4 -> x0, matrix products: 44.6 us -> none  [the longest x2 32.1 us: body(): part = jnp.dot(act, down_weights[0], preferred_element_type=jnp.float32)]
    unnamed x4 -> x1, local copies, waits for them, and re-layouts: 19.3 us -> 1.59 us
  transfers between devices with their start and end apart: 3 -> 0, of which waited for: 3 -> 0; matrix products, arithmetic and copies ran while one was open for 4% -> 0% of each run, Pallas kernels for 0% -> 0%
where the time goes in v2:
time: 102 us
  Pallas kernels  100 us (98%)
  local copies, waits for them, and re-layouts  1.59 us (2%)
    pallas_call x1, Pallas kernels, body(): pl.pallas_call(kernel, out_shape=jax.ShapeDtypeStruct(hidden_states.shape...  100 us

profile of v2, /device:TPU:1, one launch (start us, length us, event | category | flops | bytes accessed | tf_op | source)
XLA Modules:
  0.0 102.0 jit_solution(15823745237005584669)
XLA Ops:
  0.0 100.4 %shard_map.64 = bf16[2,4,7168]{2,1,0:T(4,128)(2,1)} custom-call(bf16[2,4,7168]{2,1,0:T(4,128)(2,1)} %hs.1, s32[2,4,8]{2,1,0:T(4,128)} %routes.1, bf16[2,4,8]{2,1,0:T(4,128)(2,1)} %gates.1, bf16[1,7168,256]{2,1,0:T(8,128)(2,1)} %wg_hbm.1, bf16[1,7168,256]{2,1,0:T(8,128)(2,1)} %wu_hbm.1, bf16[1,256,7168]{2,1,0:T(8,128)(2,1)} %wd_hbm.1), custom_call_target="tpu_custom_call" | custom-call | flops 11299999744 | bytes 12000000 | tf_op jit(solution)/shard_map/pallas_call | solution.py:413
  100.4 1.6 %copy.8 = bf16[2,4,7168]{2,1,0:T(4,128)(2,1)} copy(bf16[2,4,7168]{2,1,0:T(4,128)(2,1)} %shard_map.64) | data formatting | bytes 229376

commit v3 on v1

v3 whole, which is shorter than its diff:
```python
import jax
import jax.numpy as jnp
from jax import lax
from jax.experimental import pallas as pl
from jax.experimental.pallas import tpu as pltpu
from jax.sharding import PartitionSpec as P

LANE = 128
TILE = 8
UNITS = 28
HALF = UNITS * LANE
HALF_T = HALF + LANE
HIDDEN = 256
STEPS = 2
MESH = pl.DeviceIdType.MESH
F32 = jnp.float32
BF16 = jnp.bfloat16

PARTS = (
    ((0, 10, (2, 1, 0)), (10, 9, (0, 2, 1)), (19, 9, (1, 0, 2))),
    ((0, 10, (0, 2, 1)), (10, 9, (1, 0, 2)), (19, 9, (2, 1, 0))),
)
TABLE_PART = 2
N_PARTS = 3
G_SENDS, G_RECVS, B_SENDS, B_RECVS = 4, 12, 4, 15
PAIRS = tuple((s, p) for s in range(STEPS) for p in range(N_PARTS))


def part_units(q, table):
    first, count, _ = PARTS[q[0]][q[1]]
    return first, count + (1 if table and q[1] == TABLE_PART else 0)


def halves(q, table):
    first, count = part_units(q, table)
    left = (count + 1) // 2
    return (first, left), (first + left, count - left)


def kernel(
    hs, routes, gates, wg_hbm, wu_hbm, wd_hbm,
    out,
    X, wgu, wd, h, act, zero_send, zero_recv, last_send, last_recv, R0,
    *rest,
):
    n = len(PAIRS)
    R3, R2, R1 = (dict(zip(PAIRS, rest[i * n : (i + 1) * n])) for i in range(3))
    w_sem, e_send, e_recv, g_send, g_recv, b_send, b_recv = rest[3 * n :]
    core = lax.axis_index("grp")
    ep = lax.axis_index("ep")
    me = (ep // 16, (ep // 4) % 4, ep % 4)
    sibling = (1 - core, ep)
    scale = (16, 4, 1)
    parts = range(N_PARTS)

    spots = [[lax.rem(me[axis] + d, 4) for d in range(4)] for axis in range(3)]
    peers = [
        [(core, ep + (spots[axis][d] - me[axis]) * scale[axis]) for d in range(4)] for axis in range(3)
    ]

    def place(axis, delta):
        return spots[axis][delta % 4]

    def peer(axis, delta):
        return peers[axis][delta]

    weights = [
        pltpu.make_async_copy(wg_hbm.at[0], wgu.at[:, pl.ds(0, HIDDEN)], w_sem.at[0]),
        pltpu.make_async_copy(wu_hbm.at[0], wgu.at[:, pl.ds(HIDDEN, HIDDEN)], w_sem.at[1]),
        pltpu.make_async_copy(wd_hbm.at[0], wd, w_sem.at[2]),
    ]
    for copy in weights:
        copy.start()

    barrier = pltpu.get_barrier_semaphore()
    pl.semaphore_signal(barrier, inc=1, device_id=sibling, device_id_type=MESH)
    for axis in range(3):
        for delta in (2, 1, 3):
            pl.semaphore_signal(barrier, inc=1, device_id=peer(axis, delta), device_id_type=MESH)

    lane = lax.broadcasted_iota(jnp.int32, (4, LANE), 1)

    def own_rows(c):
        at = pl.multiple_of(c * HALF, LANE)
        return jnp.concatenate(
            [hs[s, :, pl.ds(at, HALF)].astype(F32) for s in range(STEPS)], axis=0
        )

    tables = []
    for s in range(STEPS):
        total = jnp.zeros((4, LANE), F32)
        for k in range(8):
            total += jnp.where(
                lane == routes[s, :, k : k + 1], gates[s, :, k : k + 1].astype(F32), 0.0
            )
        tables.append(total)
    table = jnp.concatenate(tables, axis=0)

    zero_send[:, pl.ds(0, HALF)] = own_rows(1 - core)
    zero_send[:, pl.ds(HALF, LANE)] = table
    h[...] = jnp.zeros_like(h)
    pl.semaphore_wait(barrier, 10)
    swap = pltpu.make_async_remote_copy(
        src_ref=zero_send, dst_ref=zero_recv, send_sem=e_send.at[0], recv_sem=e_recv.at[0],
        device_id=sibling, device_id_type=MESH,
    )
    swap.start()
    base = pl.multiple_of(core * HALF_T, LANE)
    mine = jnp.concatenate([own_rows(core), table], axis=1)
    first = core == 0
    swap.wait()
    theirs = zero_recv[...]
    low, high = jnp.where(first, mine, theirs), jnp.where(first, theirs, mine)
    for s in range(STEPS):
        tile = jnp.concatenate([low[4 * s : 4 * s + 4], high[4 * s : 4 * s + 4]], axis=0)
        X[s, me[0], me[1], me[2], :, pl.ds(base, HALF_T)] = tile.astype(BF16)

    def spread(q, places):
        index = [None] * 3
        for axis, j in zip(PARTS[q[0]][q[1]][2], places):
            if j is None:
                j = pl.ds(0, 4)
            index[axis] = j if isinstance(j, pl.Slice) else pl.ds(j, 1)
        return (q[0],) + tuple(index)

    def block(q, places, c, units):
        at = pl.multiple_of(c * HALF_T + units[0] * LANE, LANE)
        return spread(q, places) + (pl.ds(0, TILE), pl.ds(at, units[1] * LANE))

    def axis_of(q, n):
        return PARTS[q[0]][q[1]][2][n]

    def near(q, n, offset):
        return place(axis_of(q, n), offset)

    def index_of(q, count, k):
        return (q[0] * N_PARTS + q[1]) * count + k

    def remote(src, dst, sends, send, recvs, recv, device):
        return pltpu.make_async_remote_copy(
            src_ref=src, dst_ref=dst, send_sem=sends.at[send], recv_sem=recvs.at[recv],
            device_id=device, device_id_type=MESH,
        )

    def wait_for(ref, sem):
        pltpu.make_async_copy(ref, ref, sem).wait()

    def sized(q, places, table):
        return X.at[block(q, places, core, part_units(q, table))]

    def tiles(q, count, table):
        return sized(q, (pl.ds(0, count), 0, 0), table)

    def lines(q, count, table):
        return sized(q, (None, pl.ds(0, count), 0), table)

    def planes(q, count, table):
        return sized(q, (None, None, pl.ds(0, count)), table)

    def some(q, stage, units):
        return X.at[block(q, ((None, None, 0) if stage == 3 else (None, 0, 0)), core, units)]

    def gather_copy(q, places, units, send, recv, device):
        ref = X.at[block(q, places, core, units)]
        return remote(ref, ref, g_send, index_of(q, G_SENDS, send), g_recv, index_of(q, G_RECVS, recv), device)

    def sent(q, send, ref):
        wait_for(ref, g_send.at[index_of(q, G_SENDS, send)])

    def came(q, recv, ref):
        wait_for(ref, g_recv.at[index_of(q, G_RECVS, recv)])

    def ring(q, stage, units, offset, to, recv):
        places = (
            (None, near(q, 1, offset), near(q, 2, 0)) if stage == 2 else (None, None, near(q, 2, offset))
        )
        gather_copy(q, places, units, stage - 1, recv, peer(axis_of(q, stage - 1), to)).start()

    def passed(q, offset, recv):
        ref = X.at[block(q, (None, None, near(q, 2, offset)), core, part_units(q, False))]
        remote(
            ref, ref, g_send, index_of(q, G_SENDS, 3), g_recv, index_of(q, G_RECVS, recv), sibling
        ).start()

    def multiply(q, offsets, c):
        units = part_units(q, False)
        rows = [
            X[block(q, (None, None, near(q, 2, o)), c, units)].reshape(16 * TILE, units[1] * LANE)
            for o in offsets
        ]
        rows = rows[0] if len(rows) == 1 else jnp.concatenate(rows, axis=0)
        at = pl.multiple_of(c * HALF + units[0] * LANE, LANE)
        found = jnp.dot(rows, wgu[pl.ds(at, units[1] * LANE), :], preferred_element_type=F32)
        for i, o in enumerate(offsets):
            where = spread(q, (None, None, near(q, 2, o)))
            h[where] += found[i * 16 * TILE : (i + 1) * 16 * TILE].reshape(h[where].shape)

    def each(step):
        def over(s):
            for p in parts:
                step((s, p))
        return over

    @each
    def g1(q):
        for d in (2, 1, 3):
            places = tuple(near(q, i, 0) for i in range(3))
            gather_copy(q, places, part_units(q, True), 0, 0, peer(axis_of(q, 0), d)).start()

    @each
    def g2(q):
        came(q, 0, tiles(q, 3, True))
        a, b = halves(q, True)
        ring(q, 2, a, 0, 1, 1)
        ring(q, 2, b, 0, 3, 2)
        ring(q, 2, b, 0, 1, 3)
        ring(q, 2, a, 0, 3, 3)

    @each
    def g3(q):
        a, b = halves(q, True)
        came(q, 1, some(q, 2, a))
        ring(q, 2, a, 3, 1, 3)
        came(q, 2, some(q, 2, b))
        ring(q, 2, b, 1, 3, 3)

    @each
    def g4(q):
        came(q, 3, lines(q, 2, True))
        a, b = halves(q, True)
        ring(q, 3, a, 0, 1, 4)
        ring(q, 3, b, 0, 3, 5)
        ring(q, 3, b, 0, 1, 6)
        ring(q, 3, a, 0, 3, 6)
        passed(q, 0, 8)

    @each
    def g5(q):
        a, b = halves(q, True)
        came(q, 4, some(q, 3, a))
        ring(q, 3, a, 3, 1, 7)
        came(q, 5, some(q, 3, b))
        ring(q, 3, b, 1, 3, 7)

    @each
    def g6(q):
        came(q, 6, planes(q, 1, True))
        passed(q, 3, 9)
        passed(q, 1, 10)

    @each
    def g7(q):
        came(q, 7, planes(q, 1, True))
        passed(q, 2, 11)

    @each
    def c0(q):
        multiply(q, (0,), core)

    @each
    def c1(q):
        came(q, 8, planes(q, 1, False))
        multiply(q, (0,), 1 - core)

    @each
    def c2(q):
        multiply(q, (3, 1), core)

    @each
    def c3(q):
        came(q, 9, planes(q, 1, False))
        came(q, 10, planes(q, 1, False))
        multiply(q, (3, 1), 1 - core)

    @each
    def c4(q):
        multiply(q, (2,), core)

    @each
    def c5(q):
        came(q, 11, planes(q, 1, False))
        multiply(q, (2,), 1 - core)

    chosen = (lax.broadcasted_iota(jnp.int32, (LANE, HIDDEN), 0) == ep // 4).astype(BF16)
    table_at = pl.multiple_of(base + HALF, LANE)

    def activate(s):
        def one(i, carry):
            rows = X[s, i, :, :, :, pl.ds(table_at, LANE)].reshape(16 * TILE, LANE)
            scaled = jnp.dot(rows, chosen, preferred_element_type=F32)
            both = h[s, i].reshape(16 * TILE, 2 * HIDDEN)
            gate, up = both[:, :HIDDEN], both[:, HIDDEN:]
            value = gate / (1.0 + jnp.exp(-gate)) * up * scaled
            act[s, i] = value.astype(BF16).reshape(4, 4, TILE, HIDDEN)
            return carry

        lax.fori_loop(0, 4, one, 0)
        for p in parts:
            q = (s, p)
            sent(q, 0, tiles(q, 3, True))
            sent(q, 1, lines(q, 3, True))
            sent(q, 2, planes(q, 3, True))
            sent(q, 3, planes(q, 4, False))

    def down(q, offset, c):
        first_unit, count = part_units(q, False)
        rows = act[spread(q, (None, None, near(q, 2, offset)))].reshape(16 * TILE, HIDDEN)
        at = pl.multiple_of(c * HALF + first_unit * LANE, LANE)
        return jnp.dot(rows, wd[:, pl.ds(at, count * LANE)], preferred_element_type=F32)

    def cross_places(q, offset, c):
        units = part_units(q, False)
        places = (None, None, near(q, 2, offset))
        to = spread(q, places) + (pl.ds(0, TILE), pl.ds(units[0] * LANE, units[1] * LANE))
        return block(q, places, c, units), to

    def scatter_copy(q, src, dst, send, recv, device):
        remote(
            src, dst, b_send, index_of(q, B_SENDS, send), b_recv, index_of(q, B_RECVS, recv), device
        ).start()

    def left_off(q, send, ref):
        wait_for(ref, b_send.at[index_of(q, B_SENDS, send)])

    def landed(q, recv, ref):
        wait_for(ref, b_recv.at[index_of(q, B_RECVS, recv)])

    def theirs_out(s, offset):
        for p in parts:
            q = (s, p)
            where, to = cross_places(q, offset, 1 - core)
            X[where] = down(q, offset, 1 - core).astype(BF16).reshape(X[where].shape)
            scatter_copy(q, X.at[where], R0.at[to], 0, offset, sibling)

    def mine_out(s, offset):
        for p in parts:
            q = (s, p)
            where, to = cross_places(q, offset, core)
            found = down(q, offset, core)
            landed(q, offset, planes(q, 1, False))
            X[where] = (found.reshape(X[where].shape) + R0[to].astype(F32)).astype(BF16)
            if offset == 2:
                a, b = halves(q, False)
                ring_out(q, 3, 2, a, 0, 1, 4)
                ring_out(q, 3, 2, b, 0, 3, 5)

    def span(q, units):
        return pl.ds((units[0] - part_units(q, False)[0]) * LANE, units[1] * LANE)

    every = slice(None)

    def ring_out(q, stage, offset, units, slot, to, recv):
        places = (
            (None, near(q, 1, offset), near(q, 2, 0)) if stage == 2 else (None, None, near(q, 2, offset))
        )
        buffer = (R2 if stage == 2 else R3)[q]
        dst = buffer.at[slot, every, every, every, every, span(q, units)]
        scatter_copy(
            q, X.at[block(q, places, core, units)], dst, 1 if stage == 3 else 2, recv,
            peer(axis_of(q, stage - 1), to),
        )

    def accumulate(where, terms):
        total = X[where].astype(F32)
        for term in terms:
            total += term.astype(F32)
        X[where] = total.astype(BF16)

    @each
    def r1(q):
        a, b = halves(q, False)
        ring_out(q, 3, 1, b, 1, 1, 6)
        ring_out(q, 3, 3, a, 2, 3, 6)

    def relay(q):
        a, b = halves(q, False)
        for units, offset, recv in ((a, 1, 4), (b, 3, 5)):
            landed(q, recv, some(q, 3, units))
            term = R3[q][0, :, :, :, :, span(q, units)]
            accumulate(block(q, (None, None, near(q, 2, offset)), core, units), (term,))

    @each
    def r2(q):
        a, b = halves(q, False)
        relay(q)
        ring_out(q, 3, 1, a, 1, 1, 6)
        ring_out(q, 3, 3, b, 2, 3, 6)

    @each
    def r3(q):
        landed(q, 6, planes(q, 2, False))
        where = block(q, (None, None, near(q, 2, 0)), core, part_units(q, False))
        accumulate(where, (R3[q][1], R3[q][2]))
        a, b = halves(q, False)
        ring_out(q, 2, 2, a, 0, 1, 7)
        ring_out(q, 2, 2, b, 0, 3, 8)
        ring_out(q, 2, 1, b, 1, 1, 9)
        ring_out(q, 2, 3, a, 2, 3, 9)

    def line_index(q, line):
        return spread(q, (None, near(q, 1, line), 0))[1:]

    def r2_lines(s):
        for p in parts:
            relay((s, p))
        for line in (2, 1, 3, 0):
            for p in parts:
                q = (s, p)
                for units, offset, slot in zip(halves(q, False), (1, 3), (1, 2)):
                    src = X.at[block(q, (None, near(q, 1, line), near(q, 2, offset)), core, units)]
                    dst = R3[q].at[(slot,) + line_index(q, line) + (every, span(q, units))]
                    scatter_copy(q, src, dst, 1, 11 + line, peer(axis_of(q, 2), offset))

    def r3_lines(s):
        for p in parts:
            landed((s, p), 6, planes((s, p), 1, False))
        for line in (2, 1, 3, 0):
            for p in parts:
                q = (s, p)
                landed(q, 11 + line, lines(q, 1, False))
                where = block(q, (None, near(q, 1, line), near(q, 2, 0)), core, part_units(q, False))
                accumulate(where, tuple(R3[q][(slot,) + line_index(q, line)] for slot in (1, 2)))
                if line:
                    scatter_copy(q, X.at[where], R2[q].at[line - 1], 2, 9, peer(axis_of(q, 1), line))

    @each
    def r4(q):
        a, b = halves(q, False)
        for units, offset, slot, recv in ((a, 1, 1, 7), (b, 3, 2, 8)):
            landed(q, recv, some(q, 2, units))
            term = R2[q][0, :, :, :, :, span(q, units)]
            accumulate(block(q, (None, near(q, 1, offset), near(q, 2, 0)), core, units), (term,))
            ring_out(q, 2, offset, units, slot, offset, 9)

    @each
    def r5(q):
        units = part_units(q, False)
        if q[0] == STEPS - 1:
            landed(q, 9, lines(q, 3, False))
            terms = (R2[q][0], R2[q][1], R2[q][2])
        else:
            landed(q, 9, lines(q, 2, False))
            terms = (R2[q][1], R2[q][2])
        accumulate(block(q, (None, near(q, 1, 0), near(q, 2, 0)), core, units), terms)
        for d in (2, 1, 3):
            places = (near(q, 0, d), near(q, 1, 0), near(q, 2, 0))
            src = X.at[block(q, places, core, units)]
            scatter_copy(q, src, R1[q].at[d - 1], 3, 10, peer(axis_of(q, 0), d))

    def wait_weights(i):
        weights[i].wait()

    g1(0)
    g1(1)
    g2(0)
    g2(1)
    g3(0)
    g3(1)
    g4(0)
    wait_weights(0); wait_weights(1)
    c0(0)
    c1(0)
    g5(0)
    g4(1)
    c0(1)
    g6(0)
    c2(0)
    c3(0)
    g7(0)
    c4(0)
    c5(0)
    activate(0)
    wait_weights(2)
    theirs_out(0, 2)
    g5(1)
    mine_out(0, 2)
    theirs_out(0, 1)
    theirs_out(0, 3)
    mine_out(0, 1)
    mine_out(0, 3)
    r1(0)
    theirs_out(0, 0)
    c1(1)
    mine_out(0, 0)
    g6(1)
    c2(1)
    c3(1)
    g7(1)
    c4(1)
    c5(1)
    activate(1)
    theirs_out(1, 2)
    r2(0)
    mine_out(1, 2)
    theirs_out(1, 1)
    theirs_out(1, 3)
    mine_out(1, 1)
    mine_out(1, 3)
    r1(1)
    theirs_out(1, 0)
    mine_out(1, 0)
    r2_lines(1)
    r3(0)
    r4(0)
    r3_lines(1)
    r5(0)
    r5(1)

    kept, given = [], []
    for s in range(STEPS):
        pieces = []
        for p in parts:
            q = (s, p)
            units = part_units(q, False)
            where = block(q, tuple(near(q, i, 0) for i in range(3)), core, units)
            total = X[where].astype(F32).reshape(TILE, units[1] * LANE)
            landed(q, 10, tiles(q, 3, False))
            for d in (1, 2, 3):
                total += R1[q][d - 1].astype(F32).reshape(TILE, units[1] * LANE)
            pieces.append(total)
        tile = jnp.concatenate(pieces, axis=1)
        kept.append(jnp.where(first, tile[:4], tile[4:]))
        given.append(jnp.where(first, tile[4:], tile[:4]))
    last_send[...] = jnp.concatenate(given, axis=0)
    swap_back = pltpu.make_async_remote_copy(
        src_ref=last_send, dst_ref=last_recv, send_sem=e_send.at[1], recv_sem=e_recv.at[1],
        device_id=sibling, device_id_type=MESH,
    )
    swap_back.start()
    at = pl.multiple_of(core * HALF, LANE)
    for s in range(STEPS):
        out[s, :, pl.ds(at, HALF)] = kept[s].astype(BF16)
    for q in PAIRS:
        left_off(q, 0, planes(q, 4, False))
        left_off(q, 1, planes(q, 3, False))
        left_off(q, 2, lines(q, 3, False))
        left_off(q, 3, tiles(q, 3, False))
    swap_back.wait()
    other = last_recv[...].astype(BF16)
    at = pl.multiple_of((1 - core) * HALF, LANE)
    for s in range(STEPS):
        out[s, :, pl.ds(at, HALF)] = other[4 * s : 4 * s + 4]


def scatter_shapes():
    shapes = []
    for stage in (3, 2, 1):
        for s, p in PAIRS:
            _, count, order = PARTS[s][p]
            dims = tuple(4 if a in order[: stage - 1] else 1 for a in range(3))
            shapes.append(pltpu.VMEM((3,) + dims + (TILE, count * LANE), BF16))
    return shapes


def body(hidden_states, expert_routes, route_gates, gate_weights, up_weights, down_weights):
    width = hidden_states.shape[2]
    vmem = pl.BlockSpec(memory_space=pltpu.VMEM)
    hbm = pl.BlockSpec(memory_space=pl.ANY)
    pairs = len(PAIRS)
    copies = [
        pltpu.SemaphoreType.DMA((count,))
        for count in (3, 2, 2, *(pairs * k for k in (G_SENDS, G_RECVS, B_SENDS, B_RECVS)))
    ]
    return pl.pallas_call(
        kernel,
        out_shape=jax.ShapeDtypeStruct(hidden_states.shape, BF16),
        in_specs=[vmem, vmem, vmem, hbm, hbm, hbm],
        out_specs=vmem,
        scratch_shapes=[
            pltpu.VMEM((STEPS, 4, 4, 4, TILE, 2 * HALF_T), BF16),
            pltpu.VMEM((width, 2 * HIDDEN), BF16),
            pltpu.VMEM((HIDDEN, width), BF16),
            pltpu.VMEM((STEPS, 4, 4, 4, TILE, 2 * HIDDEN), F32),
            pltpu.VMEM((STEPS, 4, 4, 4, TILE, HIDDEN), BF16),
            pltpu.VMEM((8, HALF_T), F32),
            pltpu.VMEM((8, HALF_T), F32),
            pltpu.VMEM((8, HALF), F32),
            pltpu.VMEM((8, HALF), F32),
            pltpu.VMEM((STEPS, 4, 4, 4, TILE, HALF), BF16),
            *scatter_shapes(),
            *copies,
        ],
        compiler_params=pltpu.CompilerParams(
            collective_id=0, has_side_effects=True, vmem_limit_bytes=60 * 1024 * 1024
        ),
        cost_estimate=pl.CostEstimate(
            flops=11_300_000_000, bytes_accessed=12_000_000, transcendentals=262144
        ),
    )(hidden_states, expert_routes, route_gates, gate_weights, up_weights, down_weights)


def solution(mesh):
    return jax.shard_map(
        body,
        mesh=mesh,
        in_specs=(
            P(None, ("grp", "ep"), None),
            P(None, ("grp", "ep"), None),
            P(None, ("grp", "ep"), None),
            P("ep", None, "grp"),
            P("ep", None, "grp"),
            P("ep", "grp", None),
        ),
        out_specs=P(None, ("grp", "ep"), None),
        check_vma=False,
    )
```

time: 401 us -> 90.6 us (0.23)
  waiting for transfers between devices: 318 us -> 0 us
  Pallas kernels: 0 us -> 88.8 us
  matrix products: 44.6 us -> 0 us
  local copies, waits for them, and re-layouts: 21.2 us -> 1.59 us
  between operations: 13.2 us -> 0.01 us
    unnamed x4 -> x0, waiting for transfers between devices: 173 us -> none
    all_gather x2 -> x0, waiting for transfers between devices: 144 us -> none  [body(): full = lax.all_gather(rows[s], ('grp', 'ep'), axis=0, tiled=True)]
    pallas_call x0 -> x1, Pallas kernels: none -> 88.8 us  [body(): pl.pallas_call(kernel, out_shape=jax.ShapeDtypeStruct(hidden_states.shape...]
    dot_general x4 -> x0, matrix products: 44.6 us -> none  [the longest x2 32.1 us: body(): part = jnp.dot(act, down_weights[0], preferred_element_type=jnp.float32)]
    unnamed x4 -> x1, local copies, waits for them, and re-layouts: 19.3 us -> 1.59 us
  transfers between devices with their start and end apart: 3 -> 0, of which waited for: 3 -> 0; matrix products, arithmetic and copies ran while one was open for 4% -> 0% of each run, Pallas kernels for 0% -> 0%
where the time goes in v3:
time: 90.6 us; the launch traced here: 90.4 us
  Pallas kernels  88.8 us (98%)
  local copies, waits for them, and re-layouts  1.59 us (2%)
    pallas_call x1, Pallas kernels, body(): pl.pallas_call(kernel, out_shape=jax.ShapeDtypeStruct(hidden_states.shape...  88.8 us

profile of v3, /device:TPU:1, one launch (start us, length us, event | category | flops | bytes accessed | tf_op | source)
XLA Modules:
  0.0 90.4 jit_solution(16054983011805989581)
XLA Ops:
  0.0 88.8 %shard_map.64 = bf16[2,4,7168]{2,1,0:T(4,128)(2,1)} custom-call(bf16[2,4,7168]{2,1,0:T(4,128)(2,1)} %hs.1, s32[2,4,8]{2,1,0:T(4,128)} %routes.1, bf16[2,4,8]{2,1,0:T(4,128)(2,1)} %gates.1, bf16[1,7168,256]{2,1,0:T(8,128)(2,1)} %wg_hbm.1, bf16[1,7168,256]{2,1,0:T(8,128)(2,1)} %wu_hbm.1, bf16[1,256,7168]{2,1,0:T(8,128)(2,1)} %wd_hbm.1), custom_call_target="tpu_custom_call" | custom-call | flops 11299999744 | bytes 12000000 | tf_op jit(solution)/shard_map/pallas_call | solution.py:564
  88.8 1.6 %copy.8 = bf16[2,4,7168]{2,1,0:T(4,128)(2,1)} copy(bf16[2,4,7168]{2,1,0:T(4,128)(2,1)} %shard_map.64) | data formatting | bytes 229376

commit v4 on v3

--- a/solution.py
+++ b/solution.py
@@ -33,7 +33,7 @@
 
 def halves(q, table):
     first, count = part_units(q, table)
-    left = (count + 1) // 2
+    left = (count + 1 - q[0] % 2) // 2
     return (first, left), (first + left, count - left)
 
 
@@ -447,6 +447,29 @@
             src = X.at[block(q, places, core, units)]
             scatter_copy(q, src, R1[q].at[d - 1], 3, 10, peer(axis_of(q, 0), d))
 
+    def swap_back(s):
+        return pltpu.make_async_remote_copy(
+            src_ref=last_send.at[s], dst_ref=last_recv.at[s], send_sem=e_send.at[1 + s],
+            recv_sem=e_recv.at[1 + s], device_id=sibling, device_id_type=MESH,
+        )
+
+    def finish(s):
+        pieces = []
+        for p in parts:
+            q = (s, p)
+            units = part_units(q, False)
+            where = block(q, tuple(near(q, i, 0) for i in range(3)), core, units)
+            total = X[where].astype(F32).reshape(TILE, units[1] * LANE)
+            landed(q, 10, tiles(q, 3, False))
+            for d in (1, 2, 3):
+                total += R1[q][d - 1].astype(F32).reshape(TILE, units[1] * LANE)
+            pieces.append(total)
+        tile = jnp.concatenate(pieces, axis=1)
+        last_send[s] = jnp.where(first, tile[4:], tile[:4])
+        swap_back(s).start()
+        at = pl.multiple_of(core * HALF, LANE)
+        out[s, :, pl.ds(at, HALF)] = jnp.where(first, tile[:4], tile[4:]).astype(BF16)
+
     def wait_weights(i):
         weights[i].wait()
 
@@ -457,7 +480,8 @@
     g3(0)
     g3(1)
     g4(0)
-    wait_weights(0); wait_weights(1)
+    wait_weights(0)
+    wait_weights(1)
     c0(0)
     c1(0)
     g5(0)
@@ -472,27 +496,27 @@
     activate(0)
     wait_weights(2)
     theirs_out(0, 2)
+    theirs_out(0, 1)
     g5(1)
     mine_out(0, 2)
-    theirs_out(0, 1)
     theirs_out(0, 3)
     mine_out(0, 1)
     mine_out(0, 3)
     r1(0)
-    theirs_out(0, 0)
     c1(1)
-    mine_out(0, 0)
     g6(1)
     c2(1)
+    theirs_out(0, 0)
     c3(1)
+    mine_out(0, 0)
     g7(1)
+    r2(0)
     c4(1)
     c5(1)
     activate(1)
     theirs_out(1, 2)
-    r2(0)
+    theirs_out(1, 1)
     mine_out(1, 2)
-    theirs_out(1, 1)
     theirs_out(1, 3)
     mine_out(1, 1)
     mine_out(1, 3)
@@ -501,45 +525,22 @@
     mine_out(1, 0)
     r2_lines(1)
     r3(0)
+    r3_lines(1)
     r4(0)
-    r3_lines(1)
     r5(0)
     r5(1)
-
-    kept, given = [], []
-    for s in range(STEPS):
-        pieces = []
-        for p in parts:
-            q = (s, p)
-            units = part_units(q, False)
-            where = block(q, tuple(near(q, i, 0) for i in range(3)), core, units)
-            total = X[where].astype(F32).reshape(TILE, units[1] * LANE)
-            landed(q, 10, tiles(q, 3, False))
-            for d in (1, 2, 3):
-                total += R1[q][d - 1].astype(F32).reshape(TILE, units[1] * LANE)
-            pieces.append(total)
-        tile = jnp.concatenate(pieces, axis=1)
-        kept.append(jnp.where(first, tile[:4], tile[4:]))
-        given.append(jnp.where(first, tile[4:], tile[:4]))
-    last_send[...] = jnp.concatenate(given, axis=0)
-    swap_back = pltpu.make_async_remote_copy(
-        src_ref=last_send, dst_ref=last_recv, send_sem=e_send.at[1], recv_sem=e_recv.at[1],
-        device_id=sibling, device_id_type=MESH,
-    )
-    swap_back.start()
-    at = pl.multiple_of(core * HALF, LANE)
-    for s in range(STEPS):
-        out[s, :, pl.ds(at, HALF)] = kept[s].astype(BF16)
+    finish(0)
+    finish(1)
+
     for q in PAIRS:
         left_off(q, 0, planes(q, 4, False))
         left_off(q, 1, planes(q, 3, False))
         left_off(q, 2, lines(q, 3, False))
         left_off(q, 3, tiles(q, 3, False))
-    swap_back.wait()
-    other = last_recv[...].astype(BF16)
     at = pl.multiple_of((1 - core) * HALF, LANE)
     for s in range(STEPS):
-        out[s, :, pl.ds(at, HALF)] = other[4 * s : 4 * s + 4]
+        swap_back(s).wait()
+        out[s, :, pl.ds(at, HALF)] = last_recv[s].astype(BF16)
 
 
 def scatter_shapes():
@@ -559,7 +560,7 @@
     pairs = len(PAIRS)
     copies = [
         pltpu.SemaphoreType.DMA((count,))
-        for count in (3, 2, 2, *(pairs * k for k in (G_SENDS, G_RECVS, B_SENDS, B_RECVS)))
+        for count in (3, 3, 3, *(pairs * k for k in (G_SENDS, G_RECVS, B_SENDS, B_RECVS)))
     ]
     return pl.pallas_call(
         kernel,
@@ -574,8 +575,8 @@
             pltpu.VMEM((STEPS, 4, 4, 4, TILE, HIDDEN), BF16),
             pltpu.VMEM((8, HALF_T), F32),
             pltpu.VMEM((8, HALF_T), F32),
-            pltpu.VMEM((8, HALF), F32),
-            pltpu.VMEM((8, HALF), F32),
+            pltpu.VMEM((STEPS, 4, HALF), F32),
+            pltpu.VMEM((STEPS, 4, HALF), F32),
             pltpu.VMEM((STEPS, 4, 4, 4, TILE, HALF), BF16),
             *scatter_shapes(),
             *copies,

time: 90.6 us -> 85 us (0.938)
  Pallas kernels: 88.8 us -> 83.3 us
    pallas_call x1, Pallas kernels: 88.8 us -> 83.3 us  [body(): pl.pallas_call(kernel, out_shape=jax.ShapeDtypeStruct(hidden_states.shape...]
where the time goes in v4:
time: 85 us; the launch traced here: 84.9 us
  Pallas kernels  83.3 us (98%)
  local copies, waits for them, and re-layouts  1.59 us (2%)
    pallas_call x1, Pallas kernels, body(): pl.pallas_call(kernel, out_shape=jax.ShapeDtypeStruct(hidden_states.shape...  83.3 us

profile of v4, /device:TPU:1, one launch (start us, length us, event | category | flops | bytes accessed | tf_op | source)
XLA Modules:
  0.0 84.9 jit_solution(9418273243459030793)
XLA Ops:
  0.0 83.3 %shard_map.64 = bf16[2,4,7168]{2,1,0:T(4,128)(2,1)} custom-call(bf16[2,4,7168]{2,1,0:T(4,128)(2,1)} %hs.1, s32[2,4,8]{2,1,0:T(4,128)} %routes.1, bf16[2,4,8]{2,1,0:T(4,128)(2,1)} %gates.1, bf16[1,7168,256]{2,1,0:T(8,128)(2,1)} %wg_hbm.1, bf16[1,7168,256]{2,1,0:T(8,128)(2,1)} %wu_hbm.1, bf16[1,256,7168]{2,1,0:T(8,128)(2,1)} %wd_hbm.1), custom_call_target="tpu_custom_call" | custom-call | flops 11299999744 | bytes 12000000 | tf_op jit(solution)/shard_map/pallas_call | solution.py:565
  83.3 1.6 %copy.8 = bf16[2,4,7168]{2,1,0:T(4,128)(2,1)} copy(bf16[2,4,7168]{2,1,0:T(4,128)(2,1)} %shard_map.64) | data formatting | bytes 229376

commit v5 on v4

--- a/solution.py
+++ b/solution.py
@@ -22,7 +22,7 @@
 )
 TABLE_PART = 2
 N_PARTS = 3
-G_SENDS, G_RECVS, B_SENDS, B_RECVS = 4, 12, 4, 15
+G_SENDS, G_RECVS, B_SENDS, B_RECVS = 4, 11, 4, 15
 PAIRS = tuple((s, p) for s in range(STEPS) for p in range(N_PARTS))
 
 
@@ -246,12 +246,12 @@
     def g6(q):
         came(q, 6, planes(q, 1, True))
         passed(q, 3, 9)
-        passed(q, 1, 10)
+        passed(q, 1, 9)
 
     @each
     def g7(q):
         came(q, 7, planes(q, 1, True))
-        passed(q, 2, 11)
+        passed(q, 2, 10)
 
     @each
     def c0(q):
@@ -268,8 +268,7 @@
 
     @each
     def c3(q):
-        came(q, 9, planes(q, 1, False))
-        came(q, 10, planes(q, 1, False))
+        came(q, 9, planes(q, 2, False))
         multiply(q, (3, 1), 1 - core)
 
     @each
@@ -278,7 +277,7 @@
 
     @each
     def c5(q):
-        came(q, 11, planes(q, 1, False))
+        came(q, 10, planes(q, 1, False))
         multiply(q, (2,), 1 - core)
 
     chosen = (lax.broadcasted_iota(jnp.int32, (LANE, HIDDEN), 0) == ep // 4).astype(BF16)
@@ -302,11 +301,15 @@
             sent(q, 2, planes(q, 3, True))
             sent(q, 3, planes(q, 4, False))
 
-    def down(q, offset, c):
+    def down(q, offsets, c):
         first_unit, count = part_units(q, False)
-        rows = act[spread(q, (None, None, near(q, 2, offset)))].reshape(16 * TILE, HIDDEN)
+        rows = [
+            act[spread(q, (None, None, near(q, 2, o)))].reshape(16 * TILE, HIDDEN) for o in offsets
+        ]
+        rows = rows[0] if len(rows) == 1 else jnp.concatenate(rows, axis=0)
         at = pl.multiple_of(c * HALF + first_unit * LANE, LANE)
-        return jnp.dot(rows, wd[:, pl.ds(at, count * LANE)], preferred_element_type=F32)
+        found = jnp.dot(rows, wd[:, pl.ds(at, count * LANE)], preferred_element_type=F32)
+        return [found[i * 16 * TILE : (i + 1) * 16 * TILE] for i in range(len(offsets))]
 
     def cross_places(q, offset, c):
         units = part_units(q, False)
@@ -325,21 +328,22 @@
     def landed(q, recv, ref):
         wait_for(ref, b_recv.at[index_of(q, B_RECVS, recv)])
 
-    def theirs_out(s, offset):
+    def theirs_out(s, *offsets):
         for p in parts:
             q = (s, p)
-            where, to = cross_places(q, offset, 1 - core)
-            X[where] = down(q, offset, 1 - core).astype(BF16).reshape(X[where].shape)
-            scatter_copy(q, X.at[where], R0.at[to], 0, offset, sibling)
-
-    def mine_out(s, offset):
+            for offset, found in zip(offsets, down(q, offsets, 1 - core)):
+                where, to = cross_places(q, offset, 1 - core)
+                X[where] = found.astype(BF16).reshape(X[where].shape)
+                scatter_copy(q, X.at[where], R0.at[to], 0, offset, sibling)
+
+    def mine_out(s, *offsets):
         for p in parts:
             q = (s, p)
-            where, to = cross_places(q, offset, core)
-            found = down(q, offset, core)
-            landed(q, offset, planes(q, 1, False))
-            X[where] = (found.reshape(X[where].shape) + R0[to].astype(F32)).astype(BF16)
-            if offset == 2:
+            for offset, found in zip(offsets, down(q, offsets, core)):
+                where, to = cross_places(q, offset, core)
+                landed(q, offset, planes(q, 1, False))
+                X[where] = (found.reshape(X[where].shape) + R0[to].astype(F32)).astype(BF16)
+            if 2 in offsets:
                 a, b = halves(q, False)
                 ring_out(q, 3, 2, a, 0, 1, 4)
                 ring_out(q, 3, 2, b, 0, 3, 5)
@@ -361,6 +365,9 @@
         )
 
     def accumulate(where, terms):
+        if len(terms) == 1:
+            X[where] = X[where] + terms[0]
+            return
         total = X[where].astype(F32)
         for term in terms:
             total += term.astype(F32)
@@ -496,12 +503,10 @@
     activate(0)
     wait_weights(2)
     theirs_out(0, 2)
-    theirs_out(0, 1)
+    theirs_out(0, 1, 3)
     g5(1)
     mine_out(0, 2)
-    theirs_out(0, 3)
-    mine_out(0, 1)
-    mine_out(0, 3)
+    mine_out(0, 1, 3)
     r1(0)
     c1(1)
     g6(1)
@@ -515,11 +520,9 @@
     c5(1)
     activate(1)
     theirs_out(1, 2)
-    theirs_out(1, 1)
+    theirs_out(1, 1, 3)
     mine_out(1, 2)
-    theirs_out(1, 3)
-    mine_out(1, 1)
-    mine_out(1, 3)
+    mine_out(1, 1, 3)
     r1(1)
     theirs_out(1, 0)
     mine_out(1, 0)

time: 85 us -> 84.4 us (level)
  no operation moved by 1% of the time
where the time goes in v5:
time: 84.4 us; the launch traced here: 84.3 us
  Pallas kernels  82.7 us (98%)
  local copies, waits for them, and re-layouts  1.59 us (2%)
    pallas_call x1, Pallas kernels, body(): pl.pallas_call(kernel, out_shape=jax.ShapeDtypeStruct(hidden_states.shape...  82.7 us

profile of v5, /device:TPU:1, one launch (start us, length us, event | category | flops | bytes accessed | tf_op | source)
XLA Modules:
  0.0 84.3 jit_solution(4233106842457037710)
XLA Ops:
  0.0 82.7 %shard_map.64 = bf16[2,4,7168]{2,1,0:T(4,128)(2,1)} custom-call(bf16[2,4,7168]{2,1,0:T(4,128)(2,1)} %hs.1, s32[2,4,8]{2,1,0:T(4,128)} %routes.1, bf16[2,4,8]{2,1,0:T(4,128)(2,1)} %gates.1, bf16[1,7168,256]{2,1,0:T(8,128)(2,1)} %wg_hbm.1, bf16[1,7168,256]{2,1,0:T(8,128)(2,1)} %wu_hbm.1, bf16[1,256,7168]{2,1,0:T(8,128)(2,1)} %wd_hbm.1), custom_call_target="tpu_custom_call" | custom-call | flops 11299999744 | bytes 12000000 | tf_op jit(solution)/shard_map/pallas_call | solution.py:568
  82.7 1.6 %copy.8 = bf16[2,4,7168]{2,1,0:T(4,128)(2,1)} copy(bf16[2,4,7168]{2,1,0:T(4,128)(2,1)} %shard_map.64) | data formatting | bytes 229376
